TPU v7x, 256 devices: a whole 4x4x8 slice. The times are simulated.
256 devices in a mesh: ctx: 64 (over x, y_lo, z), tp: 4 (over y_hi, core).
Axes of the slice: x: 4, y: 4 (y_hi: 2, y_lo: 2; y = y_hi * 2 + y_lo), z: 8, core: 2. Of those that a mesh axis runs over, the one named last changes fastest.
Arguments:
- queries: bfloat16 [12288, 4096], P('ctx', 'tp'), may hold values from -40 to 40
- prompt_window_keys: bfloat16 [12288, 512], P('ctx', 'tp'), may hold values from -10 to 10
- prompt_window_values: bfloat16 [12288, 512], P('ctx', 'tp'), may hold values from -6 to 6
- stored_keys: bfloat16 [4096, 512], P('ctx', 'tp'), may hold values from -4 to 4
- stored_values: bfloat16 [4096, 512], P('ctx', 'tp'), may hold values from -6 to 6
- block_order: int32 [128], replicated, may hold values from 0 to 127, as said below
- window_offset: int32 [1], replicated, may hold values from 1024 to 4096
- out_weight: bfloat16 [4096, 4096], P('tp'), may hold values from -0.25 to 0.25
Outputs:
- projected: bfloat16 [12288, 4096], P(('ctx', 'tp'))
Inputs may be any that keep to these rules, and one draw needn't show every extreme that they name: `block_order`: block slots 2d and 2d + 1 (the rows of index d of ctx) hold two window blocks whose numbers add up to 127; every block appears once.
All inputs are finite; a program needn't handle non-finite values.
Results may differ from a plain program's by a relative error of at most 0.015.
Values may be sent and summed in bfloat16 or wider, within the bound.
No kernel may reach another device: no remote copies, remote signals or barrier semaphores. Data moves between devices by JAX's collectives and lax.ppermute only.
A program may use at most 64 MiB of HBM per device.

v0:
```python
import functools

import jax
import jax.numpy as jnp
from jax import lax
from jax.experimental import pallas as pl
from jax.experimental.pallas import tpu as pltpu
from jax.sharding import Mesh, PartitionSpec as P

HEADS = 8
D = 128
BLK = 96
TOK = 2 * BLK
CACHE = 64
SHARD = 2 * (TOK + CACHE)
ROWS = HEADS * BLK
TILE = 256
NEG = -1e30
SCALE = D**-0.5 * 1.4426950408889634
PLACE = 128
OUT_ROWS = D + 16
NT = (((1,), (1,)), ((), ()))
TN = (((0,), (0,)), ((), ()))
VMEM = pltpu.VMEM


def attend_chunk(work, sets, steps, first, last, *refs):
    refs = list(refs)

    def take(count):
        taken = refs[:count]
        del refs[:count]
        return taken

    n_query = len(work)
    (table_ref,) = take(1)
    q_refs = take(len(sets))
    msgs = take(len(steps))
    old = [] if first else take(3 * n_query)
    outs = take(n_query if last else 3 * n_query)
    m_all, l_all, acc_all, qx, kx, vx, s_a, s_b, ends, marks, item_block, item_tile = refs
    x, yl, z, offset, yh = (table_ref[PLACE + i] for i in (0, 1, 2, 3, 5))
    n_keys = 256 * 2 * len(steps)

    token = lax.broadcasted_iota(jnp.int32, (BLK, D), 0)
    column = lax.broadcasted_iota(jnp.int32, (BLK, D), 1)
    hidden = ((column < BLK) & (column > token)) | (column == BLK)
    q_extra = jnp.where(hidden, NEG, 0.0).astype(jnp.bfloat16)
    own_rows = jnp.where(column == token, 1.0, 0.0).astype(jnp.bfloat16)
    half_of = [yh if role else 1 - yh for _, role in work]
    for qb, (g, role) in enumerate(work):
        src = q_refs[sets.index(g)]
        at = pl.ds(pl.multiple_of(half_of[qb] * BLK, 32), BLK)

        def stage_head(h, carry, qb=qb, src=src, at=at):
            rows = pl.ds(pl.multiple_of(h * BLK, 32), BLK)
            qx[qb, rows, :D] = src[at, pl.ds(pl.multiple_of(h * D, D), D)]
            qx[qb, rows, D:] = q_extra
            return carry

        lax.fori_loop(0, HEADS, stage_head, 0)

    def clear(i, carry):
        rows = pl.ds(pl.multiple_of(i * D, D), D)
        kx[rows, D:] = jnp.zeros((D, D), jnp.bfloat16)
        vx[rows, :] = jnp.zeros((D, D), jnp.bfloat16)
        return carry

    def clear_keys(i, carry):
        kx[pl.ds(pl.multiple_of(i * D, D), D), :D] = jnp.zeros((D, D), jnp.bfloat16)
        return carry

    lax.fori_loop(0, kx.shape[0] // D, clear, 0)
    lax.fori_loop(n_keys // D - len(steps), kx.shape[0] // D, clear_keys, 0)

    ctxs = []
    for step in steps:
        zz = lax.rem(z + step + 8, 8)
        ctxs += [x * 16 + yl * 8 + zz, (3 - x) * 16 + yl * 8 + zz]
    cache_rows = jnp.int32(0)
    slot = lax.broadcasted_iota(jnp.int32, (CACHE, D), 0)
    lane = lax.broadcasted_iota(jnp.int32, (CACHE, D), 1)
    for j, ctx in enumerate(ctxs):
        filled = offset - ctx * CACHE
        src = msgs[j // 2]
        base = (j % 2) * SHARD

        @pl.when(filled > 0)
        def _(src=src, base=base, at=cache_rows, filled=filled):
            to = pl.ds(pl.multiple_of(at, CACHE), CACHE)
            kx[to, :D] = src[base + TOK : base + TOK + CACHE, :]
            kx[to, D:] = jnp.where((slot >= filled) & (lane == BLK), 1.0, 0.0).astype(jnp.bfloat16)
            vx[to, :] = src[base + 2 * TOK + CACHE : base + SHARD, :]

        cache_rows = cache_rows + jnp.where(filled > 0, CACHE, 0)

    ids = [table_ref[2 * ctx + b] for ctx in ctxs for b in range(2)]
    for j, mine in enumerate(ids):
        rank = jnp.int32(0)
        for k, other in enumerate(ids):
            if k != j:
                rank = rank + (other < mine).astype(jnp.int32)
        to = pl.ds(pl.multiple_of(cache_rows + rank * BLK, 32), BLK)
        src = msgs[j // 4]
        base = ((j // 2) % 2) * SHARD + (j % 2) * BLK
        kx[to, :D] = src[base : base + BLK, :]
        vx[to, :] = src[base + TOK + CACHE : base + TOK + CACHE + BLK, :]

    items = jnp.int32(0)
    for qb, (g, role) in enumerate(work):
        gx, gy = g % 2, g // 2
        q_x = x + 1 - 2 * lax.rem(x, 2) if gx else x
        q_y = 1 - yl if gy else yl
        q_id = table_ref[2 * (q_x * 16 + q_y * 8 + z) + half_of[qb]]
        count = jnp.int32(0)
        own = jnp.int32(0)
        for k in ids:
            count = count + (k <= q_id).astype(jnp.int32)
            own = own + (k == q_id).astype(jnp.int32)
        end = cache_rows + count * BLK
        ends[qb] = end
        marks[qb] = jnp.where(own > 0, end - BLK, n_keys + TILE)
        tiles = (end + TILE - 1) // TILE

        def add(t, at, qb=qb):
            item_block[at] = qb
            item_tile[at] = t
            return at + 1

        items = lax.fori_loop(0, tiles, add, items)
        if first:
            m_all[qb] = jnp.full((8, ROWS), NEG, jnp.float32)
            l_all[qb] = jnp.zeros((8, ROWS), jnp.float32)
            acc_all[qb] = jnp.zeros((D, ROWS), jnp.float32)
        else:
            m_all[qb], l_all[qb] = old[3 * qb][...], old[3 * qb + 1][...]

            def bring(i, carry, qb=qb):
                rows = pl.ds(pl.multiple_of(i * 16, 16), 16)
                acc_all[qb, rows, :] = old[3 * qb + 2][rows, :]
                return carry

            lax.fori_loop(0, D // 16, bring, 0)

    pad_lane = lax.broadcasted_iota(jnp.int32, (TILE, D), 1)
    pad_rows = jnp.where(pad_lane == BLK, 1.0, 0.0).astype(jnp.bfloat16)

    def scores(k, before):
        old, new = item_block[before], item_block[k]
        kx[pl.ds(pl.multiple_of(ends[old], 32), TILE), D:] = jnp.zeros_like(pad_rows)
        kx[pl.ds(pl.multiple_of(marks[old], 32), BLK), D:] = jnp.zeros_like(own_rows)
        kx[pl.ds(pl.multiple_of(ends[new], 32), TILE), D:] = pad_rows
        kx[pl.ds(pl.multiple_of(marks[new], 32), BLK), D:] = own_rows
        keys = kx[pl.ds(pl.multiple_of(item_tile[k] * TILE, TILE), TILE), :]
        return lax.dot_general(keys, qx[new], NT, preferred_element_type=jnp.float32)

    def absorb(s_ref, k):
        qb = item_block[k]
        s = s_ref[...]
        m0 = m_all[qb]
        m1 = jnp.maximum(m0, jnp.max(s, axis=0, keepdims=True) * SCALE)
        factor = jnp.exp2(m0 - m1)
        p = jnp.exp2(s * SCALE - m1[:1])
        l_all[qb] = l_all[qb] * factor + jnp.sum(p, axis=0, keepdims=True)
        m_all[qb] = m1
        values = vx[pl.ds(pl.multiple_of(item_tile[k] * TILE, TILE), TILE), :]
        acc_all[qb] = acc_all[qb] * factor[:1] + lax.dot_general(
            values, p.astype(jnp.bfloat16), TN, preferred_element_type=jnp.float32
        )

    @pl.when(items > 0)
    def _():
        s_a[...] = scores(0, 0)

        def pair(j, c):
            k = 2 * j
            s_b[...] = scores(k + 1, k)
            absorb(s_a, k)
            s_a[...] = scores(jnp.minimum(k + 2, items - 1), k + 1)
            absorb(s_b, k + 1)
            return c

        lax.fori_loop(0, items // 2, pair, 0)

        @pl.when(items % 2 == 1)
        def _():
            absorb(s_a, items - 1)

    for qb in range(n_query):
        if last:
            total = l_all[qb]
            some = total > 0.0
            safe = jnp.where(some, total, 1.0)
            logsum = jnp.where(some, m_all[qb] + jnp.log2(safe), NEG)
            high = logsum.astype(jnp.bfloat16)
            rest = logsum - high.astype(jnp.float32)
            mid = rest.astype(jnp.bfloat16)
            low = (rest - mid.astype(jnp.float32)).astype(jnp.bfloat16)
            row = lax.broadcasted_iota(jnp.int32, (16, ROWS), 0)
            h2, m2, l2 = (jnp.concatenate([v, v], 0).astype(jnp.float32) for v in (high, mid, low))
            outs[qb][:D, :] = (acc_all[qb] / safe[:1]).astype(jnp.bfloat16)
            outs[qb][D:, :] = jnp.where(row == 0, h2, jnp.where(row == 1, m2, l2)).astype(jnp.bfloat16)
        else:
            outs[3 * qb][...], outs[3 * qb + 1][...] = m_all[qb], l_all[qb]

            def keep(i, carry, qb=qb):
                rows = pl.ds(pl.multiple_of(i * 16, 16), 16)
                outs[3 * qb + 2][rows, :] = acc_all[qb, rows, :]
                return carry

            lax.fori_loop(0, D // 16, keep, 0)


def run_chunk(work, steps, state, last, table, queries, messages):
    first = work[0] not in state
    sets = sorted({g for g, _ in work})
    n_query = len(work)
    n_keys = 256 * 2 * len(steps)
    keep = n_keys + TILE + 128
    max_items = n_query * (n_keys // TILE + 1) + 2
    shapes = [(8, ROWS), (8, ROWS), (D, ROWS)]
    smem = pl.BlockSpec(memory_space=pltpu.SMEM)
    vmem = pl.BlockSpec(memory_space=VMEM)
    operands = [table, *(queries[g] for g in sets), *messages]
    if not first:
        operands += [array for key in work for array in state[key]]
    if last:
        out_shape = [jax.ShapeDtypeStruct((OUT_ROWS, ROWS), jnp.bfloat16)] * n_query
    else:
        out_shape = [jax.ShapeDtypeStruct(s, jnp.float32) for s in shapes] * n_query
    pairs = n_query * n_keys * ROWS * 6 // 10
    name = "_".join(["attend", *(str(g) + "AB"[role] for g, role in work), str(len(steps))])
    results = pl.pallas_call(
        functools.partial(attend_chunk, tuple(work), tuple(sets), tuple(steps), first, last),
        out_shape=out_shape,
        in_specs=[smem] + [vmem] * (len(operands) - 1),
        out_specs=[vmem] * len(out_shape),
        scratch_shapes=[VMEM((n_query, *s), jnp.float32) for s in shapes]
        + [
            VMEM((n_query, ROWS, 2 * D), jnp.bfloat16),
            VMEM((keep, 2 * D), jnp.bfloat16),
            VMEM((keep, D), jnp.bfloat16),
            VMEM((TILE, ROWS), jnp.float32),
            VMEM((TILE, ROWS), jnp.float32),
            pltpu.SMEM((8,), jnp.int32),
            pltpu.SMEM((8,), jnp.int32),
            pltpu.SMEM((max_items,), jnp.int32),
            pltpu.SMEM((max_items,), jnp.int32),
        ],
        compiler_params=pltpu.CompilerParams(vmem_limit_bytes=24 * 2**20),
        cost_estimate=pl.CostEstimate(flops=pairs * 1024, bytes_accessed=8 * 2**20, transcendentals=pairs),
        name=name,
    )(*operands)
    if last:
        return results
    for i, key in enumerate(work):
        state[key] = tuple(results[3 * i : 3 * i + 3])
    return state


def project_body(table_ref, a_ref, b_ref, c_ref, d_ref, w_ref, give_ref, mine_ref, att):
    parts = (a_ref, b_ref, c_ref, d_ref)
    logs = []
    for part in parts:
        row = part[D:, :].astype(jnp.float32)
        logs.append(row[0:1] + row[1:2] + row[2:3])
    top = functools.reduce(jnp.maximum, logs)
    weights = [jnp.exp2(v - top) for v in logs]
    share = 1.0 / sum(weights)
    mixed = sum(part[:D, :].astype(jnp.float32) * (w * share) for part, w in zip(parts, weights))
    turned = mixed.T.astype(jnp.bfloat16)
    for h in range(HEADS):
        att[:, h * D : (h + 1) * D] = turned[h * BLK : (h + 1) * BLK, :]
    core = table_ref[PLACE + 4]
    half = BLK // 2
    wide = 512

    def columns(c, carry):
        cols = pl.ds(pl.multiple_of(c * wide, wide), wide)
        full = jnp.dot(att[...], w_ref[:, cols], preferred_element_type=jnp.float32)
        give_ref[:, cols] = jnp.where(core == 0, full[half:], full[:half]).astype(jnp.bfloat16)
        mine_ref[:, cols] = jnp.where(core == 0, full[:half], full[half:])
        return carry

    lax.fori_loop(0, w_ref.shape[1] // wide, columns, 0)


def project(table, parts, weight):
    vmem = pl.BlockSpec(memory_space=VMEM)
    wide = weight.shape[1]
    return pl.pallas_call(
        project_body,
        out_shape=(
            jax.ShapeDtypeStruct((BLK // 2, wide), jnp.bfloat16),
            jax.ShapeDtypeStruct((BLK // 2, wide), jnp.float32),
        ),
        in_specs=[pl.BlockSpec(memory_space=pltpu.SMEM)] + [vmem] * 5,
        out_specs=(vmem, vmem),
        scratch_shapes=[VMEM((BLK, HEADS * D), jnp.bfloat16)],
        compiler_params=pltpu.CompilerParams(vmem_limit_bytes=24 * 2**20),
        cost_estimate=pl.CostEstimate(flops=2 * BLK * HEADS * D * wide, bytes_accessed=12 * 2**20, transcendentals=0),
        name="project",
    )(table, *parts, weight)


def total_body(a_ref, b_ref, out):
    out[...] = (a_ref[...].astype(jnp.float32) + b_ref[...].astype(jnp.float32)).astype(out.dtype)


def total(a, b, dtype):
    vmem = pl.BlockSpec(memory_space=VMEM)
    return pl.pallas_call(
        total_body,
        out_shape=jax.ShapeDtypeStruct(a.shape, dtype),
        in_specs=[vmem] * 2,
        out_specs=vmem,
        compiler_params=pltpu.CompilerParams(vmem_limit_bytes=8 * 2**20),
        name="total",
    )(a, b)


def stage_body(src, dst):
    dst[...] = src[...]


def stage(array):
    vmem = pl.BlockSpec(memory_space=VMEM)
    return pl.pallas_call(
        stage_body,
        out_shape=jax.ShapeDtypeStruct(array.shape, array.dtype),
        in_specs=[vmem],
        out_specs=vmem,
        compiler_params=pltpu.CompilerParams(vmem_limit_bytes=8 * 2**20),
        name="stage",
    )(array)


def on_device(queries, window_keys, window_values, stored_keys, stored_values, block_order, window_offset, out_weight):
    x, yl, z = lax.axis_index("x"), lax.axis_index("yl"), lax.axis_index("z")
    core, yh = lax.axis_index("core"), lax.axis_index("yh")
    place = jnp.stack([x, yl, z, window_offset[0], core, yh]).astype(jnp.int32)
    table = jnp.concatenate([block_order, place])
    shard = jnp.concatenate([window_keys, stored_keys, window_values, stored_values], 0)

    def along(array, axis, size, to):
        return lax.ppermute(array, axis, [(i, to(i)) for i in range(size)])

    shard, queries = lax.optimization_barrier((shard, queries))
    other = along(shard, "x", 4, lambda i: 3 - i)
    base = jnp.concatenate([shard, other], 0)
    pair = [(a, b) for a in range(4) for b in range(2)]
    both = [(2 * a + b, 2 * (a ^ 1) + (1 - b)) for a, b in pair]
    to_member = [
        lambda v: v,
        lambda v: along(v, "x", 4, lambda i: i ^ 1),
        lambda v: along(v, "yl", 2, lambda i: 1 - i),
        lambda v: lax.ppermute(v, ("x", "yl"), both),
    ]
    q_sets = [queries] + [to_member[g](queries) for g in (1, 2, 3)]
    up = lambda a: along(a, "z", 8, lambda i: (i + 1) % 8)
    down = lambda a: along(a, "z", 8, lambda i: (i - 1) % 8)
    base, table, q_sets[0] = lax.optimization_barrier((base, table, stage(queries)))
    a1, b1 = up(base), down(base)
    a2, b2 = up(a1), down(b1)
    state = {}
    run = lambda work, steps, messages, last=False: run_chunk(work, steps, state, last, table, q_sets, messages)
    tie = lax.optimization_barrier
    near = (0, -1, 1), (base, a1, b1)
    A, B = 0, 1
    run([(0, A), (0, B)], *near)
    run([(3, A), (3, B)], *near)
    a2, b2, state[0, A], state[3, A] = tie((a2, b2, state[0, A], state[3, A]))
    a3, b3 = up(a2), down(b2)
    far = jnp.concatenate([up(a3[:SHARD]), down(b3[SHARD:])], 0)
    run([(1, A), (1, B), (2, A), (2, B)], *near)
    run([(g, r) for r in (A, B) for g in (1, 2, 3)], (-2, 2), (a2, b2))
    end = (-3, 3, 4), (a3, b3, far)
    sent_a = run([(3, A), (1, A), (2, A)], *end, True)
    *sent_a, state[3, B] = tie((*sent_a, state[3, B]))
    got_a = [to_member[g](v) for g, v in zip((3, 1, 2), sent_a)]
    sent_b = run([(3, B), (1, B), (2, B)], *end, True)
    got_b = [to_member[g](v) for g, v in zip((3, 1, 2), sent_b)]
    *got_a, state[0, A] = tie((*got_a, state[0, A]))
    rest = (-2, 2, -3, 3, 4), (a2, b2, a3, b3, far)
    (own_a,) = run([(0, A)], *rest, True)
    swap = lambda v, axis: along(v, axis, 2, lambda i: 1 - i)
    give_a, keep_a = project(table, (own_a, *got_a), out_weight)
    give_a, *got_b = tie((give_a, *got_b))
    sum_a = total(keep_a, swap(give_a, "core"), jnp.bfloat16)
    sum_a, state[0, B] = tie((sum_a, state[0, B]))
    across = swap(sum_a, "yh")
    (own_b,) = run([(0, B)], *rest, True)
    give_b, keep_b = project(table, (own_b, *got_b), out_weight)
    keep_b = total(keep_b, across, jnp.float32)
    return (keep_b + swap(give_b, "core").astype(jnp.float32)).astype(jnp.bfloat16)


def solution(mesh):
    fine = Mesh(mesh.devices.reshape(4, 2, 8, 2, 2), ("x", "yl", "z", "yh", "core"))
    ctx, tp = ("x", "yl", "z"), ("yh", "core")
    return jax.shard_map(
        on_device,
        mesh=fine,
        in_specs=(P(ctx, tp),) * 5 + (P(), P(), P(tp, None)),
        out_specs=P((*ctx, *tp), None),
        check_vma=False,
    )
```

profile of v0, /device:TPU:1, one launch (start us, length us, event | category | flops | bytes accessed | tf_op | source)
XLA Modules:
  0.0 100.6 jit_solution(3022516570961274420)
XLA Ops:
  0.0 0.9 pad_maximum_fusion.1
  0.9 3.4 %collective-permute-start = (bf16[512,128]{1,0:T(8,128)(2,1)S(1)}, bf16[512,128]{1,0:T(8,128)(2,1)S(1)}, u32[]{:S(2)}, u32[]{:S(2)}) collective-permute-start(bf16[512,128]{1,0:T(8,128)(2,1)S(1)} %pad_maximum_fusion.1), channel_id=1, source_target_pairs={{0,192},{64,128},{128,64},{192,0},{1,193},{65,129},{129,65},{193,1... | collective-permute-start | bytes 393224 | tf_op jit(solution)/shard_map/ppermute | solution.py:346
  4.9 0.0 copy-start
  4.9 1.0 copy-done
  5.9 0.7 concatenate.14.refs_0_.table_ref
  6.7 0.0 collective-permute-done
  6.7 2.4 %collective-permute-start.1 = (bf16[1024,128]{1,0:T(8,128)(2,1)S(1)}, bf16[1024,128]{1,0:T(8,128)(2,1)S(1)}, u32[]{:S(2)}, u32[]{:S(2)}) collective-permute-start(bf16[1024,128]{1,0:T(8,128)(2,1)S(1)} %pad_maximum_fusion.refs_2_.refs_3_), channel_id=1, source_target_pairs={{0,4},{4,8},{8,12},{12,16},{16,20},{20,24},{24,28},{28,0},{1,5},{5... | collective-permute-start | bytes 786440 | tf_op jit(solution)/shard_map/ppermute | solution.py:346
  9.1 4.0 %collective-permute-start.3 = (bf16[1024,128]{1,0:T(8,128)(2,1)S(1)}, bf16[1024,128]{1,0:T(8,128)(2,1)S(1)}, u32[]{:S(2)}, u32[]{:S(2)}) collective-permute-start(bf16[1024,128]{1,0:T(8,128)(2,1)S(1)} %pad_maximum_fusion.refs_2_.refs_3_), channel_id=1, source_target_pairs={{0,28},{4,0},{8,4},{12,8},{16,12},{20,16},{24,20},{28,24},{1,29},{... | collective-permute-start | bytes 786440 | tf_op jit(solution)/shard_map/ppermute | solution.py:346
  13.1 1.0 %collective-permute-start.5 = (bf16[192,1024]{1,0:T(8,128)(2,1)}, bf16[192,1024]{1,0:T(8,128)(2,1)S(1)}, u32[]{:S(2)}, u32[]{:S(2)}) collective-permute-start(bf16[192,1024]{1,0:T(8,128)(2,1)} %src), channel_id=1, source_target_pairs={{0,96},{32,64},{64,32},{96,0},{128,224},{160,192},{192,160},{224,1... | collective-permute-start | bytes 1179656 | tf_op jit(solution)/shard_map/ppermute | solution.py:357
  14.1 1.5 %collective-permute-start.10 = (bf16[192,1024]{1,0:T(8,128)(2,1)}, bf16[192,1024]{1,0:T(8,128)(2,1)S(1)}, u32[]{:S(2)}, u32[]{:S(2)}) collective-permute-start(bf16[192,1024]{1,0:T(8,128)(2,1)} %src), channel_id=1, source_target_pairs={{0,64},{64,0},{128,192},{192,128},{1,65},{65,1},{129,193},{193,129... | collective-permute-start | bytes 1179656 | tf_op jit(solution)/shard_map/ppermute | solution.py:346
  15.6 0.2 collective-permute-start.11
  15.8 2.3 %collective-permute-done.1.refs_3_.refs_4_ = bf16[1024,128]{1,0:T(8,128)(2,1)S(1)} collective-permute-done((bf16[1024,128]{1,0:T(8,128)(2,1)S(1)}, bf16[1024,128]{1,0:T(8,128)(2,1)S(1)}, u32[]{:S(2)}, u32[]{:S(2)}) %collective-permute-start.1) | collective-permute-done | bytes 262176 | tf_op jit(solution)/shard_map/ppermute | solution.py:346
  18.1 0.0 collective-permute-start.2
  18.1 0.0 collective-permute-done.3.refs_4_.refs_5_
  18.1 2.7 %collective-permute-start.4 = (bf16[1024,128]{1,0:T(8,128)(2,1)S(1)}, bf16[1024,128]{1,0:T(8,128)(2,1)S(1)}, u32[]{:S(2)}, u32[]{:S(2)}) collective-permute-start(bf16[1024,128]{1,0:T(8,128)(2,1)S(1)} %collective-permute-done.3.refs_4_.refs_5_), channel_id=1, source_target_pairs={{0,28},{4,0},{8,4},{12,8},{16,12},{20,16},{24,20},{28,24},{1,29},{... | collective-permute-start | bytes 786440 | tf_op jit(solution)/shard_map/ppermute | solution.py:346
  20.8 4.7 %attend_0A_0B_3.1 = (f32[8,768]{1,0:T(8,128)S(1)}, f32[8,768]{1,0:T(8,128)S(1)}, f32[128,768]{1,0:T(8,128)S(1)}, f32[8,768]{1,0:T(8,128)S(1)}, f32[8,768]{1,0:T(8,128)S(1)}, /*index=5*/f32[128,768]{1,0:T(8,128)S(1)}) custom-call(s32[134]{0:T(256)S(1)} %concatenate.14.refs_0_.table_ref, bf16[192,1024]{1,0:T(8,128)(2,1)S(1)} %stage.1.refs_1_, ...), custom_call_target="tpu_custom_call" | custom-call | flops 1449550848 | bytes 8388608 | tf_op jit(solution)/shard_map/attend_0A_0B_3/pallas_call | solution.py:233
  25.5 0.0 collective-permute-done.5.refs_1_.refs_3_
  25.5 4.3 %attend_3A_3B_3.1 = (f32[8,768]{1,0:T(8,128)S(1)}, f32[8,768]{1,0:T(8,128)S(1)}, f32[128,768]{1,0:T(8,128)S(1)}, f32[8,768]{1,0:T(8,128)S(1)}, f32[8,768]{1,0:T(8,128)S(1)}, /*index=5*/f32[128,768]{1,0:T(8,128)S(1)}) custom-call(s32[134]{0:T(256)S(1)} %concatenate.14.refs_0_.table_ref, bf16[192,1024]{1,0:T(8,128)(2,1)S(1)} %collective-permute-done.5.refs_1_.refs_3_, ...), custom_call_target="tpu_custom_call" | custom-call | flops 1449550848 | bytes 8388608 | tf_op jit(solution)/shard_map/attend_3A_3B_3/pallas_call | solution.py:233
  29.8 0.0 collective-permute-done.2.refs_4_.refs_2_
  29.8 0.0 collective-permute-done.4.refs_5_.refs_3_
  29.8 0.1 collective-permute-start.6
  29.9 2.7 %collective-permute-start.7 = (bf16[1024,128]{1,0:T(8,128)(2,1)S(1)}, bf16[1024,128]{1,0:T(8,128)(2,1)S(1)}, u32[]{:S(2)}, u32[]{:S(2)}) collective-permute-start(bf16[1024,128]{1,0:T(8,128)(2,1)S(1)} %collective-permute-done.4.refs_5_.refs_3_), channel_id=1, source_target_pairs={{0,28},{4,0},{8,4},{12,8},{16,12},{20,16},{24,20},{28,24},{1,29},{... | collective-permute-start | bytes 786440 | tf_op jit(solution)/shard_map/ppermute | solution.py:346
  32.5 0.0 collective-permute-done.10.refs_1_
  32.5 1.1 %collective-permute-done.11.refs_2_ = bf16[192,1024]{1,0:T(8,128)(2,1)S(1)} collective-permute-done((bf16[192,1024]{1,0:T(8,128)(2,1)}, bf16[192,1024]{1,0:T(8,128)(2,1)S(1)}, u32[]{:S(2)}, u32[]{:S(2)}) %collective-permute-start.11) | collective-permute-done | bytes 393248 | tf_op jit(solution)/shard_map/ppermute | solution.py:346
  33.7 7.3 %attend_1A_1B_2A_2B_3.1 = (f32[8,768]{1,0:T(8,128)S(1)}, f32[8,768]{1,0:T(8,128)S(1)}, f32[128,768]{1,0:T(8,128)S(1)}, f32[8,768]{1,0:T(8,128)S(1)}, f32[8,768]{...) custom-call(s32[134]{0:T(256)S(1)} %concatenate.14.refs_0_.table_ref, ...), custom_call_target="tpu_custom_call" | custom-call | flops 2899102720 | bytes 8388608 | tf_op jit(solution)/shard_map/attend_1A_1B_2A_2B_3/pallas_call | solution.py:233
  41.0 0.0 collective-permute-done.6.refs_4_
  41.0 0.3 collective-permute-start.8
  41.3 0.0 collective-permute-done.7.refs_5_
  41.3 2.7 %collective-permute-start.9 = (bf16[512,128]{1,0:T(8,128)(2,1)S(1)}, bf16[512,128]{1,0:T(8,128)(2,1)S(1)}, u32[]{:S(2)}, u32[]{:S(2)}) collective-permute-start(bf16[512,128]{1,0:T(8,128)(2,1)S(1)} %slice.9), channel_id=1, source_target_pairs={{0,28},{4,0},{8,4},{12,8},{16,12},{20,16},{24,20},{28,24},{1,29},{... | collective-permute-start | bytes 393224 | tf_op jit(solution)/shard_map/ppermute | solution.py:346
  44.0 8.2 %attend_1A_2A_3A_1B_2B_3B_2.1 = (f32[8,768]{1,0:T(8,128)S(1)}, f32[8,768]{1,0:T(8,128)S(1)}, f32[128,768]{1,0:T(8,128)S(1)}, f32[8,768]{1,0:T(8,128)S(1)}, f32[8...) custom-call(s32[134]{0:T(256)S(1)} %concatenate.14.refs_0_.table_ref, ...), custom_call_target="tpu_custom_call" | custom-call | flops 2899102720 | bytes 8388608 | tf_op jit(solution)/shard_map/attend_1A_2A_3A_1B_2B_3B_2/pallas_call | solution.py:233
  52.2 0.0 collective-permute-done.8
  52.3 0.0 collective-permute-done.9
  52.3 0.0 slice-start
  52.3 4.3 %attend_3A_1A_2A_3.1 = (bf16[144,768]{1,0:T(8,128)(2,1)S(1)}, bf16[144,768]{1,0:T(8,128)(2,1)S(1)}, bf16[144,768]{1,0:T(8,128)(2,1)S(1)}) custom-call(s32[134]{0:T(256)S(1)} %concatenate.14.refs_0_.table_ref, bf16[192,1024]{1,0:T(8,128)(2,1)S(1)} %collective-permute-done.10.refs_1_, bf16[192,1024]{1,0:T(8,128)(2,1)S(1)} %collective-permute-done.11.refs_2_, ...), custom_call_target="tpu_custom_call" | custom-call | flops 2174326784 | bytes 8388608 | tf_op jit(solution)/shard_map/attend_3A_1A_2A_3/pallas_call | solution.py:233
  56.6 2.6 %collective-permute-start.12 = (bf16[144,768]{1,0:T(8,128)(2,1)S(1)}, bf16[144,768]{1,0:T(8,128)(2,1)S(1)}, u32[]{:S(2)}, u32[]{:S(2)}) collective-permute-start(bf16[144,768]{1,0:T(8,128)(2,1)S(1)} %get-tuple-element.136), channel_id=1, source_target_pairs={{0,96},{32,64},{64,32},{96,0},{128,224},{160,192},{192,160},{224,1... | collective-permute-start | bytes 663560 | tf_op jit(solution)/shard_map/ppermute | solution.py:357
  59.2 1.8 %collective-permute-start.13 = (bf16[144,768]{1,0:T(8,128)(2,1)S(1)}, bf16[144,768]{1,0:T(8,128)(2,1)S(1)}, u32[]{:S(2)}, u32[]{:S(2)}) collective-permute-start(bf16[144,768]{1,0:T(8,128)(2,1)S(1)} %get-tuple-element.137), channel_id=1, source_target_pairs={{0,64},{64,0},{128,192},{192,128},{1,65},{65,1},{129,193},{193,129... | collective-permute-start | bytes 663560 | tf_op jit(solution)/shard_map/ppermute | solution.py:346
  61.0 1.1 %collective-permute-start.14 = (bf16[144,768]{1,0:T(8,128)(2,1)S(1)}, bf16[144,768]{1,0:T(8,128)(2,1)S(1)}, u32[]{:S(2)}, u32[]{:S(2)}) collective-permute-start(bf16[144,768]{1,0:T(8,128)(2,1)S(1)} %get-tuple-element.138), channel_id=1, source_target_pairs={{0,32},{32,0},{1,33},{33,1},{2,34},{34,2},{3,35},{35,3},{4,36},{36... | collective-permute-start | bytes 663560 | tf_op jit(solution)/shard_map/ppermute | solution.py:346
  62.1 0.0 slice-start.1
  62.1 7.6 %attend_3B_1B_2B_3.1 = (bf16[144,768]{1,0:T(8,128)(2,1)S(1)}, bf16[144,768]{1,0:T(8,128)(2,1)S(1)}, bf16[144,768]{1,0:T(8,128)(2,1)S(1)}) custom-call(s32[134]{0:T(256)S(1)} %concatenate.14.refs_0_.table_ref, bf16[192,1024]{1,0:T(8,128)(2,1)S(1)} %collective-permute-done.10.refs_1_, bf16[192,1024]{1,0:T(8,128)(2,1)S(1)} %collective-permute-done.11.refs_2_, ...), custom_call_target="tpu_custom_call" | custom-call | flops 2174326784 | bytes 8388608 | tf_op jit(solution)/shard_map/attend_3B_1B_2B_3/pallas_call | solution.py:233
  69.7 0.1 collective-permute-start.15
  69.8 0.5 collective-permute-start.16
  70.3 0.0 collective-permute-done.12.b_ref
  70.3 2.2 %collective-permute-start.17 = (bf16[144,768]{1,0:T(8,128)(2,1)S(1)}, bf16[144,768]{1,0:T(8,128)(2,1)S(1)}, u32[]{:S(2)}, u32[]{:S(2)}) collective-permute-start(bf16[144,768]{1,0:T(8,128)(2,1)S(1)} %get-tuple-element.161), channel_id=1, source_target_pairs={{0,32},{32,0},{1,33},{33,1},{2,34},{34,2},{3,35},{35,3},{4,36},{36... | collective-permute-start | bytes 663560 | tf_op jit(solution)/shard_map/ppermute | solution.py:346
  72.4 0.0 collective-permute-done.13.c_ref
  72.4 0.0 collective-permute-done.14.d_ref
  72.4 5.6 %attend_0A_5.1.a_ref = bf16[144,768]{1,0:T(8,128)(2,1)S(1)} custom-call(s32[134]{0:T(256)S(1)} %concatenate.14.refs_0_.table_ref, bf16[192,1024]{1,0:T(8,128)(2,1)S(1)} %stage.1.refs_1_, bf16[1024,128]{1,0:T(8,128)(2,1)S(1)} %collective-permute-done.2.refs_4_.refs_2_, bf16[1024,128]{1,0:T(8,128)(2,1)S(1)} %collective-permute-done.4.refs_5_.refs_3_, ...), custom_call_target="tpu_custom_call" | custom-call | flops 1207959552 | bytes 8388608 | tf_op jit(solution)/shard_map/attend_0A_5/pallas_call | solution.py:233
  78.1 0.0 slice-done
  78.1 0.0 slice-done.1
  78.1 3.3 %project.2 = (bf16[48,4096]{1,0:T(8,128)(2,1)S(1)}, f32[48,4096]{1,0:T(8,128)S(1)}) custom-call(s32[134]{0:T(256)S(1)} %concatenate.14.refs_0_.table_ref, bf16[144,768]{1,0:T(8,128)(2,1)S(1)} %attend_0A_5.1.a_ref, bf16[144,768]{1,0:T(8,128)(2,1)S(1)} %collective-permute-done.12.b_ref, bf16[144,768]{1,0:T(8,128)(2,1)S(1)} %collective-permute-done.13.c_ref, ...), custom_call_target="tpu_custom_call" | custom-call | flops 805306368 | bytes 12582912 | tf_op jit(solution)/shard_map/project/pallas_call | solution.py:291
  81.4 0.0 collective-permute-done.15.b_ref
  81.4 0.0 collective-permute-done.16.c_ref
  81.5 0.0 collective-permute-done.17.d_ref
  81.5 4.8 %collective-permute-start.18 = (bf16[48,4096]{1,0:T(8,128)(2,1)S(1)}, bf16[48,4096]{1,0:T(8,128)(2,1)S(1)}, u32[]{:S(2)}, u32[]{:S(2)}) collective-permute-start(bf16[48,4096]{1,0:T(8,128)(2,1)S(1)} %get-tuple-element.162), channel_id=1, source_target_pairs={{0,1},{1,0},{2,3},{3,2},{4,5},{5,4},{6,7},{7,6},{8,9},{9,8},{10,11... | collective-permute-start | bytes 1179656 | tf_op jit(solution)/shard_map/ppermute | solution.py:346
  86.3 1.3 %collective-permute-done.18.b_ref = bf16[48,4096]{1,0:T(8,128)(2,1)S(1)} collective-permute-done((bf16[48,4096]{1,0:T(8,128)(2,1)S(1)}, bf16[48,4096]{1,0:T(8,128)(2,1)S(1)}, u32[]{:S(2)}, u32[]{:S(2)}) %collective-permute-start.18) | collective-permute-done | bytes 393248 | tf_op jit(solution)/shard_map/ppermute | solution.py:346
  87.6 0.1 total.2
  87.7 1.4 %collective-permute-start.19 = (bf16[48,4096]{1,0:T(8,128)(2,1)S(1)}, bf16[48,4096]{1,0:T(8,128)(2,1)S(1)}, u32[]{:S(2)}, u32[]{:S(2)}) collective-permute-start(bf16[48,4096]{1,0:T(8,128)(2,1)S(1)} %total.2), channel_id=1, source_target_pairs={{0,2},{2,0},{1,3},{3,1},{4,6},{6,4},{5,7},{7,5},{8,10},{10,8},{9,1... | collective-permute-start | bytes 1179656 | tf_op jit(solution)/shard_map/ppermute | solution.py:346
  89.1 2.8 %attend_0B_5.1.a_ref = bf16[144,768]{1,0:T(8,128)(2,1)S(1)} custom-call(s32[134]{0:T(256)S(1)} %concatenate.14.refs_0_.table_ref, bf16[192,1024]{1,0:T(8,128)(2,1)S(1)} %stage.1.refs_1_, bf16[1024,128]{1,0:T(8,128)(2,1)S(1)} %collective-permute-done.2.refs_4_.refs_2_, bf16[1024,128]{1,0:T(8,128)(2,1)S(1)} %collective-permute-done.4.refs_5_.refs_3_, ...), custom_call_target="tpu_custom_call" | custom-call | flops 1207959552 | bytes 8388608 | tf_op jit(solution)/shard_map/attend_0B_5/pallas_call | solution.py:233
  92.0 3.3 %project.3 = (bf16[48,4096]{1,0:T(8,128)(2,1)S(1)}, f32[48,4096]{1,0:T(8,128)S(1)}) custom-call(s32[134]{0:T(256)S(1)} %concatenate.14.refs_0_.table_ref, bf16[144,768]{1,0:T(8,128)(2,1)S(1)} %attend_0B_5.1.a_ref, bf16[144,768]{1,0:T(8,128)(2,1)S(1)} %collective-permute-done.15.b_ref, bf16[144,768]{1,0:T(8,128)(2,1)S(1)} %collective-permute-done.16.c_ref, ...), custom_call_target="tpu_custom_call" | custom-call | flops 805306368 | bytes 12582912 | tf_op jit(solution)/shard_map/project/pallas_call | solution.py:291
  95.3 0.8 collective-permute-start.20
  96.1 3.6 %collective-permute-done.19.b_ref = bf16[48,4096]{1,0:T(8,128)(2,1)S(1)} collective-permute-done((bf16[48,4096]{1,0:T(8,128)(2,1)S(1)}, bf16[48,4096]{1,0:T(8,128)(2,1)S(1)}, u32[]{:S(2)}, u32[]{:S(2)}) %collective-permute-start.19) | collective-permute-done | bytes 393248 | tf_op jit(solution)/shard_map/ppermute | solution.py:346
  99.6 0.1 total.3
  99.7 0.0 collective-permute-done.20
  99.7 0.8 add_convert_fusion
  (7 shorter events, 0.1 us)
Async XLA Ops:
  0.9 5.8 %collective-permute-start = (bf16[512,128]{1,0:T(8,128)(2,1)S(1)}, bf16[512,128]{1,0:T(8,128)(2,1)S(1)}, u32[]{:S(2)}, u32[]{:S(2)}) collective-permute-start(bf16[512,128]{1,0:T(8,128)(2,1)S(1)} %pad_maximum_fusion.1), channel_id=1, source_target_pairs={{0,192},{64,128},{128,64},{192,0},{1,193},{65,129},{129,65},{193,1... | collective-permute-start | bytes 393224 | tf_op jit(solution)/shard_map/ppermute | solution.py:346
  4.9 1.0 copy-start
  6.7 11.4 %collective-permute-start.1 = (bf16[1024,128]{1,0:T(8,128)(2,1)S(1)}, bf16[1024,128]{1,0:T(8,128)(2,1)S(1)}, u32[]{:S(2)}, u32[]{:S(2)}) collective-permute-start(bf16[1024,128]{1,0:T(8,128)(2,1)S(1)} %pad_maximum_fusion.refs_2_.refs_3_), channel_id=1, source_target_pairs={{0,4},{4,8},{8,12},{12,16},{16,20},{20,24},{24,28},{28,0},{1,5},{5... | collective-permute-start | bytes 786440 | tf_op jit(solution)/shard_map/ppermute | solution.py:346
  9.1 9.0 %collective-permute-start.3 = (bf16[1024,128]{1,0:T(8,128)(2,1)S(1)}, bf16[1024,128]{1,0:T(8,128)(2,1)S(1)}, u32[]{:S(2)}, u32[]{:S(2)}) collective-permute-start(bf16[1024,128]{1,0:T(8,128)(2,1)S(1)} %pad_maximum_fusion.refs_2_.refs_3_), channel_id=1, source_target_pairs={{0,28},{4,0},{8,4},{12,8},{16,12},{20,16},{24,20},{28,24},{1,29},{... | collective-permute-start | bytes 786440 | tf_op jit(solution)/shard_map/ppermute | solution.py:346
  13.1 12.3 %collective-permute-start.5 = (bf16[192,1024]{1,0:T(8,128)(2,1)}, bf16[192,1024]{1,0:T(8,128)(2,1)S(1)}, u32[]{:S(2)}, u32[]{:S(2)}) collective-permute-start(bf16[192,1024]{1,0:T(8,128)(2,1)} %src), channel_id=1, source_target_pairs={{0,96},{32,64},{64,32},{96,0},{128,224},{160,192},{192,160},{224,1... | collective-permute-start | bytes 1179656 | tf_op jit(solution)/shard_map/ppermute | solution.py:357
  14.1 18.4 %collective-permute-start.10 = (bf16[192,1024]{1,0:T(8,128)(2,1)}, bf16[192,1024]{1,0:T(8,128)(2,1)S(1)}, u32[]{:S(2)}, u32[]{:S(2)}) collective-permute-start(bf16[192,1024]{1,0:T(8,128)(2,1)} %src), channel_id=1, source_target_pairs={{0,64},{64,0},{128,192},{192,128},{1,65},{65,1},{129,193},{193,129... | collective-permute-start | bytes 1179656 | tf_op jit(solution)/shard_map/ppermute | solution.py:346
  15.6 18.1 %collective-permute-start.11 = (bf16[192,1024]{1,0:T(8,128)(2,1)}, bf16[192,1024]{1,0:T(8,128)(2,1)S(1)}, u32[]{:S(2)}, u32[]{:S(2)}) collective-permute-start(bf16[192,1024]{1,0:T(8,128)(2,1)} %src), channel_id=1, source_target_pairs={{0,32},{32,0},{1,33},{33,1},{2,34},{34,2},{3,35},{35,3},{4,36},{36... | collective-permute-start | bytes 1179656 | tf_op jit(solution)/shard_map/ppermute | solution.py:346
  18.1 11.7 %collective-permute-start.2 = (bf16[1024,128]{1,0:T(8,128)(2,1)S(1)}, bf16[1024,128]{1,0:T(8,128)(2,1)S(1)}, u32[]{:S(2)}, u32[]{:S(2)}) collective-permute-start(bf16[1024,128]{1,0:T(8,128)(2,1)S(1)} %collective-permute-done.1.refs_3_.refs_4_), channel_id=1, source_target_pairs={{0,4},{4,8},{8,12},{12,16},{16,20},{20,24},{24,28},{28,0},{1,5},{5... | collective-permute-start | bytes 786440 | tf_op jit(solution)/shard_map/ppermute | solution.py:346
  18.1 11.7 %collective-permute-start.4 = (bf16[1024,128]{1,0:T(8,128)(2,1)S(1)}, bf16[1024,128]{1,0:T(8,128)(2,1)S(1)}, u32[]{:S(2)}, u32[]{:S(2)}) collective-permute-start(bf16[1024,128]{1,0:T(8,128)(2,1)S(1)} %collective-permute-done.3.refs_4_.refs_5_), channel_id=1, source_target_pairs={{0,28},{4,0},{8,4},{12,8},{16,12},{20,16},{24,20},{28,24},{1,29},{... | collective-permute-start | bytes 786440 | tf_op jit(solution)/shard_map/ppermute | solution.py:346
  29.8 11.2 %collective-permute-start.6 = (bf16[1024,128]{1,0:T(8,128)(2,1)S(1)}, bf16[1024,128]{1,0:T(8,128)(2,1)S(1)}, u32[]{:S(2)}, u32[]{:S(2)}) collective-permute-start(bf16[1024,128]{1,0:T(8,128)(2,1)S(1)} %collective-permute-done.2.refs_4_.refs_2_), channel_id=1, source_target_pairs={{0,4},{4,8},{8,12},{12,16},{16,20},{20,24},{24,28},{28,0},{1,5},{5... | collective-permute-start | bytes 786440 | tf_op jit(solution)/shard_map/ppermute | solution.py:346
  29.9 11.4 %collective-permute-start.7 = (bf16[1024,128]{1,0:T(8,128)(2,1)S(1)}, bf16[1024,128]{1,0:T(8,128)(2,1)S(1)}, u32[]{:S(2)}, u32[]{:S(2)}) collective-permute-start(bf16[1024,128]{1,0:T(8,128)(2,1)S(1)} %collective-permute-done.4.refs_5_.refs_3_), channel_id=1, source_target_pairs={{0,28},{4,0},{8,4},{12,8},{16,12},{20,16},{24,20},{28,24},{1,29},{... | collective-permute-start | bytes 786440 | tf_op jit(solution)/shard_map/ppermute | solution.py:346
  41.0 11.2 %collective-permute-start.8 = (bf16[512,128]{1,0:T(8,128)(2,1)S(1)}, bf16[512,128]{1,0:T(8,128)(2,1)S(1)}, u32[]{:S(2)}, u32[]{:S(2)}) collective-permute-start(bf16[512,128]{1,0:T(8,128)(2,1)S(1)} %slice.8), channel_id=1, source_target_pairs={{0,4},{4,8},{8,12},{12,16},{16,20},{20,24},{24,28},{28,0},{1,5},{5... | collective-permute-start | bytes 393224 | tf_op jit(solution)/shard_map/ppermute | solution.py:346
  41.3 11.0 %collective-permute-start.9 = (bf16[512,128]{1,0:T(8,128)(2,1)S(1)}, bf16[512,128]{1,0:T(8,128)(2,1)S(1)}, u32[]{:S(2)}, u32[]{:S(2)}) collective-permute-start(bf16[512,128]{1,0:T(8,128)(2,1)S(1)} %slice.9), channel_id=1, source_target_pairs={{0,28},{4,0},{8,4},{12,8},{16,12},{20,16},{24,20},{28,24},{1,29},{... | collective-permute-start | bytes 393224 | tf_op jit(solution)/shard_map/ppermute | solution.py:346
  52.3 25.8 %slice-start = ((s8[8388608]{0:T(1024)(128)(4,1)}), s8[4194304]{0:T(1024)(128)(4,1)S(1)}, s32[]{:S(2)}) async-start(s8[8388608]{0:T(1024)(128)(4,1)} %bitcast.5), calls=%async_computation | async-start | bytes 8388608
  56.6 13.6 %collective-permute-start.12 = (bf16[144,768]{1,0:T(8,128)(2,1)S(1)}, bf16[144,768]{1,0:T(8,128)(2,1)S(1)}, u32[]{:S(2)}, u32[]{:S(2)}) collective-permute-start(bf16[144,768]{1,0:T(8,128)(2,1)S(1)} %get-tuple-element.136), channel_id=1, source_target_pairs={{0,96},{32,64},{64,32},{96,0},{128,224},{160,192},{192,160},{224,1... | collective-permute-start | bytes 663560 | tf_op jit(solution)/shard_map/ppermute | solution.py:357
  59.2 13.2 %collective-permute-start.13 = (bf16[144,768]{1,0:T(8,128)(2,1)S(1)}, bf16[144,768]{1,0:T(8,128)(2,1)S(1)}, u32[]{:S(2)}, u32[]{:S(2)}) collective-permute-start(bf16[144,768]{1,0:T(8,128)(2,1)S(1)} %get-tuple-element.137), channel_id=1, source_target_pairs={{0,64},{64,0},{128,192},{192,128},{1,65},{65,1},{129,193},{193,129... | collective-permute-start | bytes 663560 | tf_op jit(solution)/shard_map/ppermute | solution.py:346
  61.0 11.4 %collective-permute-start.14 = (bf16[144,768]{1,0:T(8,128)(2,1)S(1)}, bf16[144,768]{1,0:T(8,128)(2,1)S(1)}, u32[]{:S(2)}, u32[]{:S(2)}) collective-permute-start(bf16[144,768]{1,0:T(8,128)(2,1)S(1)} %get-tuple-element.138), channel_id=1, source_target_pairs={{0,32},{32,0},{1,33},{33,1},{2,34},{34,2},{3,35},{35,3},{4,36},{36... | collective-permute-start | bytes 663560 | tf_op jit(solution)/shard_map/ppermute | solution.py:346
  62.1 16.0 %slice-start.1 = ((s8[8388608]{0:T(1024)(128)(4,1)}), s8[4194304]{0:T(1024)(128)(4,1)S(1)}, s32[]{:S(2)}) async-start(s8[8388608]{0:T(1024)(128)(4,1)} %bitcast.5), calls=%async_computation.1 | async-start | bytes 8388608
  69.7 11.8 %collective-permute-start.15 = (bf16[144,768]{1,0:T(8,128)(2,1)S(1)}, bf16[144,768]{1,0:T(8,128)(2,1)S(1)}, u32[]{:S(2)}, u32[]{:S(2)}) collective-permute-start(bf16[144,768]{1,0:T(8,128)(2,1)S(1)} %get-tuple-element.159), channel_id=1, source_target_pairs={{0,96},{32,64},{64,32},{96,0},{128,224},{160,192},{192,160},{224,1... | collective-permute-start | bytes 663560 | tf_op jit(solution)/shard_map/ppermute | solution.py:357
  69.8 11.7 %collective-permute-start.16 = (bf16[144,768]{1,0:T(8,128)(2,1)S(1)}, bf16[144,768]{1,0:T(8,128)(2,1)S(1)}, u32[]{:S(2)}, u32[]{:S(2)}) collective-permute-start(bf16[144,768]{1,0:T(8,128)(2,1)S(1)} %get-tuple-element.160), channel_id=1, source_target_pairs={{0,64},{64,0},{128,192},{192,128},{1,65},{65,1},{129,193},{193,129... | collective-permute-start | bytes 663560 | tf_op jit(solution)/shard_map/ppermute | solution.py:346
  70.3 11.2 %collective-permute-start.17 = (bf16[144,768]{1,0:T(8,128)(2,1)S(1)}, bf16[144,768]{1,0:T(8,128)(2,1)S(1)}, u32[]{:S(2)}, u32[]{:S(2)}) collective-permute-start(bf16[144,768]{1,0:T(8,128)(2,1)S(1)} %get-tuple-element.161), channel_id=1, source_target_pairs={{0,32},{32,0},{1,33},{33,1},{2,34},{34,2},{3,35},{35,3},{4,36},{36... | collective-permute-start | bytes 663560 | tf_op jit(solution)/shard_map/ppermute | solution.py:346
  81.5 6.2 %collective-permute-start.18 = (bf16[48,4096]{1,0:T(8,128)(2,1)S(1)}, bf16[48,4096]{1,0:T(8,128)(2,1)S(1)}, u32[]{:S(2)}, u32[]{:S(2)}) collective-permute-start(bf16[48,4096]{1,0:T(8,128)(2,1)S(1)} %get-tuple-element.162), channel_id=1, source_target_pairs={{0,1},{1,0},{2,3},{3,2},{4,5},{5,4},{6,7},{7,6},{8,9},{9,8},{10,11... | collective-permute-start | bytes 1179656 | tf_op jit(solution)/shard_map/ppermute | solution.py:346
  87.7 11.9 %collective-permute-start.19 = (bf16[48,4096]{1,0:T(8,128)(2,1)S(1)}, bf16[48,4096]{1,0:T(8,128)(2,1)S(1)}, u32[]{:S(2)}, u32[]{:S(2)}) collective-permute-start(bf16[48,4096]{1,0:T(8,128)(2,1)S(1)} %total.2), channel_id=1, source_target_pairs={{0,2},{2,0},{1,3},{3,1},{4,6},{6,4},{5,7},{7,5},{8,10},{10,8},{9,1... | collective-permute-start | bytes 1179656 | tf_op jit(solution)/shard_map/ppermute | solution.py:346
  95.3 4.4 %collective-permute-start.20 = (bf16[48,4096]{1,0:T(8,128)(2,1)S(1)}, bf16[48,4096]{1,0:T(8,128)(2,1)S(1)}, u32[]{:S(2)}, u32[]{:S(2)}) collective-permute-start(bf16[48,4096]{1,0:T(8,128)(2,1)S(1)} %get-tuple-element.174), channel_id=1, source_target_pairs={{0,1},{1,0},{2,3},{3,2},{4,5},{5,4},{6,7},{7,6},{8,9},{9,8},{10,11... | collective-permute-start | bytes 1179656 | tf_op jit(solution)/shard_map/ppermute | solution.py:346
where the time goes:
time: 101 us
  Pallas kernels  51.6 us (51%)
  starting transfers between devices  36.1 us (36%)
  waiting for transfers between devices  8.45 us (8%)
  local copies, waits for them, and re-layouts  1.79 us (2%)
  other arithmetic  1.7 us (2%)
    pallas_call x8, Pallas kernels, run_chunk(): pl.pallas_call(functools.partial(attend_chunk, tuple(work), tuple(sets),...  44.8 us
    ppermute x18, starting transfers between devices, along(): return lax.ppermute(array, axis, [(i, to(i)) for i in range(size)])  32.4 us
    ppermute x18, waiting for transfers between devices, along(): return lax.ppermute(array, axis, [(i, to(i)) for i in range(size)])  8.44 us
    pallas_call x2, Pallas kernels, project(): pl.pallas_call(project_body, out_shape=(jax.ShapeDtypeStruct((BLK // 2, w...  6.64 us
    ppermute x3, starting transfers between devices, on_device(): lax.ppermute(v, ('x', 'yl'), both)  3.68 us
  transfers between devices with their start and end apart: 21, of which 4 were waited for; matrix products, arithmetic and copies ran while one was open for 1% of the time, Pallas kernels for 47%

commit v1 on v0

--- a/solution.py
+++ b/solution.py
@@ -14,7 +14,7 @@
 CACHE = 64
 SHARD = 2 * (TOK + CACHE)
 ROWS = HEADS * BLK
-TILE = 256
+TILE = 384
 NEG = -1e30
 SCALE = D**-0.5 * 1.4426950408889634
 PLACE = 128
@@ -95,11 +95,13 @@
         cache_rows = cache_rows + jnp.where(filled > 0, CACHE, 0)
 
     ids = [table_ref[2 * ctx + b] for ctx in ctxs for b in range(2)]
-    for j, mine in enumerate(ids):
-        rank = jnp.int32(0)
-        for k, other in enumerate(ids):
-            if k != j:
-                rank = rank + (other < mine).astype(jnp.int32)
+    ranks = [jnp.int32(0)] * len(ids)
+    for j in range(len(ids)):
+        for k in range(j):
+            below = (ids[k] < ids[j]).astype(jnp.int32)
+            ranks[j] = ranks[j] + below
+            ranks[k] = ranks[k] + 1 - below
+    for j, rank in enumerate(ranks):
         to = pl.ds(pl.multiple_of(cache_rows + rank * BLK, 32), BLK)
         src = msgs[j // 4]
         base = ((j // 2) % 2) * SHARD + (j % 2) * BLK
@@ -176,15 +178,25 @@
             k = 2 * j
             s_b[...] = scores(k + 1, k)
             absorb(s_a, k)
-            s_a[...] = scores(jnp.minimum(k + 2, items - 1), k + 1)
+            s_a[...] = scores(k + 2, k + 1)
             absorb(s_b, k + 1)
             return c
 
-        lax.fori_loop(0, items // 2, pair, 0)
-
-        @pl.when(items % 2 == 1)
+        lax.fori_loop(0, (items - 1) // 2, pair, 0)
+
+        @pl.when(items % 2 == 0)
         def _():
-            absorb(s_a, items - 1)
+            s_b[...] = scores(items - 1, items - 2)
+            absorb(s_a, items - 2)
+
+            def hand(i, c):
+                rows = pl.ds(pl.multiple_of(i * 64, 64), 64)
+                s_a[rows, :] = s_b[rows, :]
+                return c
+
+            lax.fori_loop(0, TILE // 64, hand, 0)
+
+        absorb(s_a, items - 1)
 
     for qb in range(n_query):
         if last:

time: 101 us -> 98.6 us (0.976); the launches traced: 101 us -> 97 us
  Pallas kernels: 51.6 us -> 48 us
  waiting for transfers between devices: 8.45 us -> 7.05 us
  starting transfers between devices: 36.1 us -> 37.5 us
    pallas_call x8, Pallas kernels: 44.8 us -> 41.2 us  [run_chunk(): pl.pallas_call(functools.partial(attend_chunk, tuple(work), tuple(sets),...]
    ppermute x3, starting transfers between devices: 3.68 us -> 6.96 us  [on_device(): lax.ppermute(v, ('x', 'yl'), both)]
    ppermute x18, starting transfers between devices: 32.4 us -> 30.5 us  [along(): return lax.ppermute(array, axis, [(i, to(i)) for i in range(size)])]
    ppermute x18, waiting for transfers between devices: 8.44 us -> 7.04 us  [along(): return lax.ppermute(array, axis, [(i, to(i)) for i in range(size)])]
  transfers between devices with their start and end apart: 21 -> 21, of which waited for: 4 -> 5; matrix products, arithmetic and copies ran while one was open for 1% -> 1% of each run, Pallas kernels for 47% -> 45%
where the time goes in v1:
time: 98.6 us; the launch traced here: 97 us
  Pallas kernels  48 us (49%)
  starting transfers between devices  37.5 us (38%)
  waiting for transfers between devices  7.05 us (7%)
  local copies, waits for them, and re-layouts  1.79 us (2%)
  other arithmetic  1.7 us (2%)
    pallas_call x8, Pallas kernels, run_chunk(): pl.pallas_call(functools.partial(attend_chunk, tuple(work), tuple(sets),...  41.2 us
    ppermute x18, starting transfers between devices, along(): return lax.ppermute(array, axis, [(i, to(i)) for i in range(size)])  30.5 us
    ppermute x18, waiting for transfers between devices, along(): return lax.ppermute(array, axis, [(i, to(i)) for i in range(size)])  7.04 us
    ppermute x3, starting transfers between devices, on_device(): lax.ppermute(v, ('x', 'yl'), both)  6.96 us
    pallas_call x2, Pallas kernels, project(): pl.pallas_call(project_body, out_shape=(jax.ShapeDtypeStruct((BLK // 2, w...  6.63 us
  transfers between devices with their start and end apart: 21, of which 5 were waited for; matrix products, arithmetic and copies ran while one was open for 1% of the time, Pallas kernels for 45%

profile of v1, /device:TPU:1, one launch (start us, length us, event | category | flops | bytes accessed | tf_op | source)
XLA Modules:
  0.0 97.0 jit_solution(11559919352259499880)
XLA Ops:
  0.0 0.9 pad_maximum_fusion.1
  0.9 3.4 %collective-permute-start = (bf16[512,128]{1,0:T(8,128)(2,1)S(1)}, bf16[512,128]{1,0:T(8,128)(2,1)S(1)}, u32[]{:S(2)}, u32[]{:S(2)}) collective-permute-start(bf16[512,128]{1,0:T(8,128)(2,1)S(1)} %pad_maximum_fusion.1), channel_id=1, source_target_pairs={{0,192},{64,128},{128,64},{192,0},{1,193},{65,129},{129,65},{193,1... | collective-permute-start | bytes 393224 | tf_op jit(solution)/shard_map/ppermute | solution.py:358
  4.9 0.0 copy-start
  4.9 1.0 %copy-done = bf16[192,1024]{1,0:T(8,128)(2,1)S(1)} copy-done((bf16[192,1024]{1,0:T(8,128)(2,1)S(1)}, bf16[192,1024]{1,0:T(8,128)(2,1)}, u32[]{:S(2)}) %copy-start) | copy-done | bytes 393240
  5.9 0.7 concatenate.14.refs_0_.table_ref
  6.7 0.0 collective-permute-done
  6.7 2.4 %collective-permute-start.1 = (bf16[1024,128]{1,0:T(8,128)(2,1)S(1)}, bf16[1024,128]{1,0:T(8,128)(2,1)S(1)}, u32[]{:S(2)}, u32[]{:S(2)}) collective-permute-start(bf16[1024,128]{1,0:T(8,128)(2,1)S(1)} %pad_maximum_fusion.refs_2_.refs_3_), channel_id=1, source_target_pairs={{0,4},{4,8},{8,12},{12,16},{16,20},{20,24},{24,28},{28,0},{1,5},{5... | collective-permute-start | bytes 786440 | tf_op jit(solution)/shard_map/ppermute | solution.py:358
  9.1 4.0 %collective-permute-start.3 = (bf16[1024,128]{1,0:T(8,128)(2,1)S(1)}, bf16[1024,128]{1,0:T(8,128)(2,1)S(1)}, u32[]{:S(2)}, u32[]{:S(2)}) collective-permute-start(bf16[1024,128]{1,0:T(8,128)(2,1)S(1)} %pad_maximum_fusion.refs_2_.refs_3_), channel_id=1, source_target_pairs={{0,28},{4,0},{8,4},{12,8},{16,12},{20,16},{24,20},{28,24},{1,29},{... | collective-permute-start | bytes 786440 | tf_op jit(solution)/shard_map/ppermute | solution.py:358
  13.1 1.0 %collective-permute-start.5 = (bf16[192,1024]{1,0:T(8,128)(2,1)}, bf16[192,1024]{1,0:T(8,128)(2,1)S(1)}, u32[]{:S(2)}, u32[]{:S(2)}) collective-permute-start(bf16[192,1024]{1,0:T(8,128)(2,1)} %src), channel_id=1, source_target_pairs={{0,96},{32,64},{64,32},{96,0},{128,224},{160,192},{192,160},{224,1... | collective-permute-start | bytes 1179656 | tf_op jit(solution)/shard_map/ppermute | solution.py:369
  14.1 1.5 %collective-permute-start.10 = (bf16[192,1024]{1,0:T(8,128)(2,1)}, bf16[192,1024]{1,0:T(8,128)(2,1)S(1)}, u32[]{:S(2)}, u32[]{:S(2)}) collective-permute-start(bf16[192,1024]{1,0:T(8,128)(2,1)} %src), channel_id=1, source_target_pairs={{0,64},{64,0},{128,192},{192,128},{1,65},{65,1},{129,193},{193,129... | collective-permute-start | bytes 1179656 | tf_op jit(solution)/shard_map/ppermute | solution.py:358
  15.6 0.2 collective-permute-start.11
  15.8 2.3 %collective-permute-done.1.refs_3_.refs_4_ = bf16[1024,128]{1,0:T(8,128)(2,1)S(1)} collective-permute-done((bf16[1024,128]{1,0:T(8,128)(2,1)S(1)}, bf16[1024,128]{1,0:T(8,128)(2,1)S(1)}, u32[]{:S(2)}, u32[]{:S(2)}) %collective-permute-start.1) | collective-permute-done | bytes 262176 | tf_op jit(solution)/shard_map/ppermute | solution.py:358
  18.1 0.0 collective-permute-start.2
  18.1 0.0 collective-permute-done.3.refs_4_.refs_5_
  18.1 2.7 %collective-permute-start.4 = (bf16[1024,128]{1,0:T(8,128)(2,1)S(1)}, bf16[1024,128]{1,0:T(8,128)(2,1)S(1)}, u32[]{:S(2)}, u32[]{:S(2)}) collective-permute-start(bf16[1024,128]{1,0:T(8,128)(2,1)S(1)} %collective-permute-done.3.refs_4_.refs_5_), channel_id=1, source_target_pairs={{0,28},{4,0},{8,4},{12,8},{16,12},{20,16},{24,20},{28,24},{1,29},{... | collective-permute-start | bytes 786440 | tf_op jit(solution)/shard_map/ppermute | solution.py:358
  20.8 4.0 %attend_0A_0B_3.1 = (f32[8,768]{1,0:T(8,128)S(1)}, f32[8,768]{1,0:T(8,128)S(1)}, f32[128,768]{1,0:T(8,128)S(1)}, f32[8,768]{1,0:T(8,128)S(1)}, f32[8,768]{1,0:T(8,128)S(1)}, /*index=5*/f32[128,768]{1,0:T(8,128)S(1)}) custom-call(s32[134]{0:T(256)S(1)} %concatenate.14.refs_0_.table_ref, bf16[192,1024]{1,0:T(8,128)(2,1)S(1)} %stage.1.refs_1_, ...), custom_call_target="tpu_custom_call" | custom-call | flops 1449550848 | bytes 8388608 | tf_op jit(solution)/shard_map/attend_0A_0B_3/pallas_call | solution.py:245
  24.8 0.0 collective-permute-done.5.refs_1_.refs_3_
  24.8 4.0 %attend_3A_3B_3.1 = (f32[8,768]{1,0:T(8,128)S(1)}, f32[8,768]{1,0:T(8,128)S(1)}, f32[128,768]{1,0:T(8,128)S(1)}, f32[8,768]{1,0:T(8,128)S(1)}, f32[8,768]{1,0:T(8,128)S(1)}, /*index=5*/f32[128,768]{1,0:T(8,128)S(1)}) custom-call(s32[134]{0:T(256)S(1)} %concatenate.14.refs_0_.table_ref, bf16[192,1024]{1,0:T(8,128)(2,1)S(1)} %collective-permute-done.5.refs_1_.refs_3_, ...), custom_call_target="tpu_custom_call" | custom-call | flops 1449550848 | bytes 8388608 | tf_op jit(solution)/shard_map/attend_3A_3B_3/pallas_call | solution.py:245
  28.8 0.0 collective-permute-done.2.refs_4_.refs_2_
  28.9 0.0 collective-permute-done.4.refs_5_.refs_3_
  28.9 0.1 collective-permute-start.6
  29.0 2.7 %collective-permute-start.7 = (bf16[1024,128]{1,0:T(8,128)(2,1)S(1)}, bf16[1024,128]{1,0:T(8,128)(2,1)S(1)}, u32[]{:S(2)}, u32[]{:S(2)}) collective-permute-start(bf16[1024,128]{1,0:T(8,128)(2,1)S(1)} %collective-permute-done.4.refs_5_.refs_3_), channel_id=1, source_target_pairs={{0,28},{4,0},{8,4},{12,8},{16,12},{20,16},{24,20},{28,24},{1,29},{... | collective-permute-start | bytes 786440 | tf_op jit(solution)/shard_map/ppermute | solution.py:358
  31.6 0.0 collective-permute-done.10.refs_1_
  31.6 2.1 %collective-permute-done.11.refs_2_ = bf16[192,1024]{1,0:T(8,128)(2,1)S(1)} collective-permute-done((bf16[192,1024]{1,0:T(8,128)(2,1)}, bf16[192,1024]{1,0:T(8,128)(2,1)S(1)}, u32[]{:S(2)}, u32[]{:S(2)}) %collective-permute-start.11) | collective-permute-done | bytes 393248 | tf_op jit(solution)/shard_map/ppermute | solution.py:358
  33.7 6.4 %attend_1A_1B_2A_2B_3.1 = (f32[8,768]{1,0:T(8,128)S(1)}, f32[8,768]{1,0:T(8,128)S(1)}, f32[128,768]{1,0:T(8,128)S(1)}, f32[8,768]{1,0:T(8,128)S(1)}, f32[8,768]{...) custom-call(s32[134]{0:T(256)S(1)} %concatenate.14.refs_0_.table_ref, ...), custom_call_target="tpu_custom_call" | custom-call | flops 2899102720 | bytes 8388608 | tf_op jit(solution)/shard_map/attend_1A_1B_2A_2B_3/pallas_call | solution.py:245
  40.1 0.0 collective-permute-done.6.refs_4_
  40.2 0.1 collective-permute-start.8
  40.2 0.0 collective-permute-done.7.refs_5_
  40.3 2.7 %collective-permute-start.9 = (bf16[512,128]{1,0:T(8,128)(2,1)S(1)}, bf16[512,128]{1,0:T(8,128)(2,1)S(1)}, u32[]{:S(2)}, u32[]{:S(2)}) collective-permute-start(bf16[512,128]{1,0:T(8,128)(2,1)S(1)} %slice.9), channel_id=1, source_target_pairs={{0,28},{4,0},{8,4},{12,8},{16,12},{20,16},{24,20},{28,24},{1,29},{... | collective-permute-start | bytes 393224 | tf_op jit(solution)/shard_map/ppermute | solution.py:358
  43.0 7.4 %attend_1A_2A_3A_1B_2B_3B_2.1 = (f32[8,768]{1,0:T(8,128)S(1)}, f32[8,768]{1,0:T(8,128)S(1)}, f32[128,768]{1,0:T(8,128)S(1)}, f32[8,768]{1,0:T(8,128)S(1)}, f32[8...) custom-call(s32[134]{0:T(256)S(1)} %concatenate.14.refs_0_.table_ref, ...), custom_call_target="tpu_custom_call" | custom-call | flops 2899102720 | bytes 8388608 | tf_op jit(solution)/shard_map/attend_1A_2A_3A_1B_2B_3B_2/pallas_call | solution.py:245
  50.4 0.0 collective-permute-done.8
  50.4 0.0 collective-permute-done.9
  50.5 0.0 slice-start
  50.5 4.3 %attend_3A_1A_2A_3.1 = (bf16[144,768]{1,0:T(8,128)(2,1)S(1)}, bf16[144,768]{1,0:T(8,128)(2,1)S(1)}, bf16[144,768]{1,0:T(8,128)(2,1)S(1)}) custom-call(s32[134]{0:T(256)S(1)} %concatenate.14.refs_0_.table_ref, bf16[192,1024]{1,0:T(8,128)(2,1)S(1)} %collective-permute-done.10.refs_1_, bf16[192,1024]{1,0:T(8,128)(2,1)S(1)} %collective-permute-done.11.refs_2_, ...), custom_call_target="tpu_custom_call" | custom-call | flops 2174326784 | bytes 8388608 | tf_op jit(solution)/shard_map/attend_3A_1A_2A_3/pallas_call | solution.py:245
  54.8 3.8 %collective-permute-start.12 = (bf16[144,768]{1,0:T(8,128)(2,1)S(1)}, bf16[144,768]{1,0:T(8,128)(2,1)S(1)}, u32[]{:S(2)}, u32[]{:S(2)}) collective-permute-start(bf16[144,768]{1,0:T(8,128)(2,1)S(1)} %get-tuple-element.136), channel_id=1, source_target_pairs={{0,96},{32,64},{64,32},{96,0},{128,224},{160,192},{192,160},{224,1... | collective-permute-start | bytes 663560 | tf_op jit(solution)/shard_map/ppermute | solution.py:369
  58.6 0.0 collective-permute-start.13
  58.6 0.6 collective-permute-start.14
  59.2 0.0 slice-start.1
  59.2 6.9 %attend_3B_1B_2B_3.1 = (bf16[144,768]{1,0:T(8,128)(2,1)S(1)}, bf16[144,768]{1,0:T(8,128)(2,1)S(1)}, bf16[144,768]{1,0:T(8,128)(2,1)S(1)}) custom-call(s32[134]{0:T(256)S(1)} %concatenate.14.refs_0_.table_ref, bf16[192,1024]{1,0:T(8,128)(2,1)S(1)} %collective-permute-done.10.refs_1_, bf16[192,1024]{1,0:T(8,128)(2,1)S(1)} %collective-permute-done.11.refs_2_, ...), custom_call_target="tpu_custom_call" | custom-call | flops 2174326784 | bytes 8388608 | tf_op jit(solution)/shard_map/attend_3B_1B_2B_3/pallas_call | solution.py:245
  66.1 2.2 %collective-permute-start.15 = (bf16[144,768]{1,0:T(8,128)(2,1)S(1)}, bf16[144,768]{1,0:T(8,128)(2,1)S(1)}, u32[]{:S(2)}, u32[]{:S(2)}) collective-permute-start(bf16[144,768]{1,0:T(8,128)(2,1)S(1)} %get-tuple-element.159), channel_id=1, source_target_pairs={{0,96},{32,64},{64,32},{96,0},{128,224},{160,192},{192,160},{224,1... | collective-permute-start | bytes 663560 | tf_op jit(solution)/shard_map/ppermute | solution.py:369
  68.2 0.0 collective-permute-start.16
  68.3 0.0 collective-permute-done.12.b_ref
  68.3 0.6 collective-permute-start.17
  68.8 0.0 collective-permute-done.13.c_ref
  68.8 0.0 collective-permute-done.14.d_ref
  68.8 4.1 %attend_0A_5.1.a_ref = bf16[144,768]{1,0:T(8,128)(2,1)S(1)} custom-call(s32[134]{0:T(256)S(1)} %concatenate.14.refs_0_.table_ref, bf16[192,1024]{1,0:T(8,128)(2,1)S(1)} %stage.1.refs_1_, bf16[1024,128]{1,0:T(8,128)(2,1)S(1)} %collective-permute-done.2.refs_4_.refs_2_, bf16[1024,128]{1,0:T(8,128)(2,1)S(1)} %collective-permute-done.4.refs_5_.refs_3_, ...), custom_call_target="tpu_custom_call" | custom-call | flops 1207959552 | bytes 8388608 | tf_op jit(solution)/shard_map/attend_0A_5/pallas_call | solution.py:245
  72.9 0.0 slice-done
  72.9 0.0 slice-done.1
  72.9 3.3 %project.2 = (bf16[48,4096]{1,0:T(8,128)(2,1)S(1)}, f32[48,4096]{1,0:T(8,128)S(1)}) custom-call(s32[134]{0:T(256)S(1)} %concatenate.14.refs_0_.table_ref, bf16[144,768]{1,0:T(8,128)(2,1)S(1)} %attend_0A_5.1.a_ref, bf16[144,768]{1,0:T(8,128)(2,1)S(1)} %collective-permute-done.12.b_ref, bf16[144,768]{1,0:T(8,128)(2,1)S(1)} %collective-permute-done.13.c_ref, ...), custom_call_target="tpu_custom_call" | custom-call | flops 805306368 | bytes 12582912 | tf_op jit(solution)/shard_map/project/pallas_call | solution.py:303
  76.3 0.0 collective-permute-done.15.b_ref
  76.3 0.0 collective-permute-done.16.c_ref
  76.3 0.0 collective-permute-done.17.d_ref
  76.3 4.3 %collective-permute-start.18 = (bf16[48,4096]{1,0:T(8,128)(2,1)S(1)}, bf16[48,4096]{1,0:T(8,128)(2,1)S(1)}, u32[]{:S(2)}, u32[]{:S(2)}) collective-permute-start(bf16[48,4096]{1,0:T(8,128)(2,1)S(1)} %get-tuple-element.162), channel_id=1, source_target_pairs={{0,1},{1,0},{2,3},{3,2},{4,5},{5,4},{6,7},{7,6},{8,9},{9,8},{10,11... | collective-permute-start | bytes 1179656 | tf_op jit(solution)/shard_map/ppermute | solution.py:358
  80.6 1.3 %collective-permute-done.18.b_ref = bf16[48,4096]{1,0:T(8,128)(2,1)S(1)} collective-permute-done((bf16[48,4096]{1,0:T(8,128)(2,1)S(1)}, bf16[48,4096]{1,0:T(8,128)(2,1)S(1)}, u32[]{:S(2)}, u32[]{:S(2)}) %collective-permute-start.18) | collective-permute-done | bytes 393248 | tf_op jit(solution)/shard_map/ppermute | solution.py:358
  82.0 0.1 total.2
  82.1 4.6 %collective-permute-start.19 = (bf16[48,4096]{1,0:T(8,128)(2,1)S(1)}, bf16[48,4096]{1,0:T(8,128)(2,1)S(1)}, u32[]{:S(2)}, u32[]{:S(2)}) collective-permute-start(bf16[48,4096]{1,0:T(8,128)(2,1)S(1)} %total.2), channel_id=1, source_target_pairs={{0,2},{2,0},{1,3},{3,1},{4,6},{6,4},{5,7},{7,5},{8,10},{10,8},{9,1... | collective-permute-start | bytes 1179656 | tf_op jit(solution)/shard_map/ppermute | solution.py:358
  86.7 4.1 %attend_0B_5.1.a_ref = bf16[144,768]{1,0:T(8,128)(2,1)S(1)} custom-call(s32[134]{0:T(256)S(1)} %concatenate.14.refs_0_.table_ref, bf16[192,1024]{1,0:T(8,128)(2,1)S(1)} %stage.1.refs_1_, bf16[1024,128]{1,0:T(8,128)(2,1)S(1)} %collective-permute-done.2.refs_4_.refs_2_, bf16[1024,128]{1,0:T(8,128)(2,1)S(1)} %collective-permute-done.4.refs_5_.refs_3_, ...), custom_call_target="tpu_custom_call" | custom-call | flops 1207959552 | bytes 8388608 | tf_op jit(solution)/shard_map/attend_0B_5/pallas_call | solution.py:245
  90.7 3.3 %project.3 = (bf16[48,4096]{1,0:T(8,128)(2,1)S(1)}, f32[48,4096]{1,0:T(8,128)S(1)}) custom-call(s32[134]{0:T(256)S(1)} %concatenate.14.refs_0_.table_ref, bf16[144,768]{1,0:T(8,128)(2,1)S(1)} %attend_0B_5.1.a_ref, bf16[144,768]{1,0:T(8,128)(2,1)S(1)} %collective-permute-done.15.b_ref, bf16[144,768]{1,0:T(8,128)(2,1)S(1)} %collective-permute-done.16.c_ref, ...), custom_call_target="tpu_custom_call" | custom-call | flops 805306368 | bytes 12582912 | tf_op jit(solution)/shard_map/project/pallas_call | solution.py:303
  94.1 0.7 collective-permute-start.20
  94.8 1.1 %collective-permute-done.19.b_ref = bf16[48,4096]{1,0:T(8,128)(2,1)S(1)} collective-permute-done((bf16[48,4096]{1,0:T(8,128)(2,1)S(1)}, bf16[48,4096]{1,0:T(8,128)(2,1)S(1)}, u32[]{:S(2)}, u32[]{:S(2)}) %collective-permute-start.19) | collective-permute-done | bytes 393248 | tf_op jit(solution)/shard_map/ppermute | solution.py:358
  95.9 0.1 total.3
  96.0 0.2 collective-permute-done.20
  96.1 0.8 add_convert_fusion
  (7 shorter events, 0.1 us)
Async XLA Ops:
  0.9 5.8 %collective-permute-start = (bf16[512,128]{1,0:T(8,128)(2,1)S(1)}, bf16[512,128]{1,0:T(8,128)(2,1)S(1)}, u32[]{:S(2)}, u32[]{:S(2)}) collective-permute-start(bf16[512,128]{1,0:T(8,128)(2,1)S(1)} %pad_maximum_fusion.1), channel_id=1, source_target_pairs={{0,192},{64,128},{128,64},{192,0},{1,193},{65,129},{129,65},{193,1... | collective-permute-start | bytes 393224 | tf_op jit(solution)/shard_map/ppermute | solution.py:358
  4.9 1.0 %copy-start = (bf16[192,1024]{1,0:T(8,128)(2,1)S(1)}, bf16[192,1024]{1,0:T(8,128)(2,1)}, u32[]{:S(2)}) copy-start(bf16[192,1024]{1,0:T(8,128)(2,1)} %src) | copy-start | bytes 1179652
  6.7 11.4 %collective-permute-start.1 = (bf16[1024,128]{1,0:T(8,128)(2,1)S(1)}, bf16[1024,128]{1,0:T(8,128)(2,1)S(1)}, u32[]{:S(2)}, u32[]{:S(2)}) collective-permute-start(bf16[1024,128]{1,0:T(8,128)(2,1)S(1)} %pad_maximum_fusion.refs_2_.refs_3_), channel_id=1, source_target_pairs={{0,4},{4,8},{8,12},{12,16},{16,20},{20,24},{24,28},{28,0},{1,5},{5... | collective-permute-start | bytes 786440 | tf_op jit(solution)/shard_map/ppermute | solution.py:358
  9.1 9.0 %collective-permute-start.3 = (bf16[1024,128]{1,0:T(8,128)(2,1)S(1)}, bf16[1024,128]{1,0:T(8,128)(2,1)S(1)}, u32[]{:S(2)}, u32[]{:S(2)}) collective-permute-start(bf16[1024,128]{1,0:T(8,128)(2,1)S(1)} %pad_maximum_fusion.refs_2_.refs_3_), channel_id=1, source_target_pairs={{0,28},{4,0},{8,4},{12,8},{16,12},{20,16},{24,20},{28,24},{1,29},{... | collective-permute-start | bytes 786440 | tf_op jit(solution)/shard_map/ppermute | solution.py:358
  13.1 11.7 %collective-permute-start.5 = (bf16[192,1024]{1,0:T(8,128)(2,1)}, bf16[192,1024]{1,0:T(8,128)(2,1)S(1)}, u32[]{:S(2)}, u32[]{:S(2)}) collective-permute-start(bf16[192,1024]{1,0:T(8,128)(2,1)} %src), channel_id=1, source_target_pairs={{0,96},{32,64},{64,32},{96,0},{128,224},{160,192},{192,160},{224,1... | collective-permute-start | bytes 1179656 | tf_op jit(solution)/shard_map/ppermute | solution.py:369
  14.1 17.5 %collective-permute-start.10 = (bf16[192,1024]{1,0:T(8,128)(2,1)}, bf16[192,1024]{1,0:T(8,128)(2,1)S(1)}, u32[]{:S(2)}, u32[]{:S(2)}) collective-permute-start(bf16[192,1024]{1,0:T(8,128)(2,1)} %src), channel_id=1, source_target_pairs={{0,64},{64,0},{128,192},{192,128},{1,65},{65,1},{129,193},{193,129... | collective-permute-start | bytes 1179656 | tf_op jit(solution)/shard_map/ppermute | solution.py:358
  15.6 18.1 %collective-permute-start.11 = (bf16[192,1024]{1,0:T(8,128)(2,1)}, bf16[192,1024]{1,0:T(8,128)(2,1)S(1)}, u32[]{:S(2)}, u32[]{:S(2)}) collective-permute-start(bf16[192,1024]{1,0:T(8,128)(2,1)} %src), channel_id=1, source_target_pairs={{0,32},{32,0},{1,33},{33,1},{2,34},{34,2},{3,35},{35,3},{4,36},{36... | collective-permute-start | bytes 1179656 | tf_op jit(solution)/shard_map/ppermute | solution.py:358
  18.1 10.7 %collective-permute-start.2 = (bf16[1024,128]{1,0:T(8,128)(2,1)S(1)}, bf16[1024,128]{1,0:T(8,128)(2,1)S(1)}, u32[]{:S(2)}, u32[]{:S(2)}) collective-permute-start(bf16[1024,128]{1,0:T(8,128)(2,1)S(1)} %collective-permute-done.1.refs_3_.refs_4_), channel_id=1, source_target_pairs={{0,4},{4,8},{8,12},{12,16},{16,20},{20,24},{24,28},{28,0},{1,5},{5... | collective-permute-start | bytes 786440 | tf_op jit(solution)/shard_map/ppermute | solution.py:358
  18.1 10.7 %collective-permute-start.4 = (bf16[1024,128]{1,0:T(8,128)(2,1)S(1)}, bf16[1024,128]{1,0:T(8,128)(2,1)S(1)}, u32[]{:S(2)}, u32[]{:S(2)}) collective-permute-start(bf16[1024,128]{1,0:T(8,128)(2,1)S(1)} %collective-permute-done.3.refs_4_.refs_5_), channel_id=1, source_target_pairs={{0,28},{4,0},{8,4},{12,8},{16,12},{20,16},{24,20},{28,24},{1,29},{... | collective-permute-start | bytes 786440 | tf_op jit(solution)/shard_map/ppermute | solution.py:358
  28.9 11.3 %collective-permute-start.6 = (bf16[1024,128]{1,0:T(8,128)(2,1)S(1)}, bf16[1024,128]{1,0:T(8,128)(2,1)S(1)}, u32[]{:S(2)}, u32[]{:S(2)}) collective-permute-start(bf16[1024,128]{1,0:T(8,128)(2,1)S(1)} %collective-permute-done.2.refs_4_.refs_2_), channel_id=1, source_target_pairs={{0,4},{4,8},{8,12},{12,16},{16,20},{20,24},{24,28},{28,0},{1,5},{5... | collective-permute-start | bytes 786440 | tf_op jit(solution)/shard_map/ppermute | solution.py:358
  29.0 11.3 %collective-permute-start.7 = (bf16[1024,128]{1,0:T(8,128)(2,1)S(1)}, bf16[1024,128]{1,0:T(8,128)(2,1)S(1)}, u32[]{:S(2)}, u32[]{:S(2)}) collective-permute-start(bf16[1024,128]{1,0:T(8,128)(2,1)S(1)} %collective-permute-done.4.refs_5_.refs_3_), channel_id=1, source_target_pairs={{0,28},{4,0},{8,4},{12,8},{16,12},{20,16},{24,20},{28,24},{1,29},{... | collective-permute-start | bytes 786440 | tf_op jit(solution)/shard_map/ppermute | solution.py:358
  40.2 10.2 %collective-permute-start.8 = (bf16[512,128]{1,0:T(8,128)(2,1)S(1)}, bf16[512,128]{1,0:T(8,128)(2,1)S(1)}, u32[]{:S(2)}, u32[]{:S(2)}) collective-permute-start(bf16[512,128]{1,0:T(8,128)(2,1)S(1)} %slice.8), channel_id=1, source_target_pairs={{0,4},{4,8},{8,12},{12,16},{16,20},{20,24},{24,28},{28,0},{1,5},{5... | collective-permute-start | bytes 393224 | tf_op jit(solution)/shard_map/ppermute | solution.py:358
  40.3 10.1 %collective-permute-start.9 = (bf16[512,128]{1,0:T(8,128)(2,1)S(1)}, bf16[512,128]{1,0:T(8,128)(2,1)S(1)}, u32[]{:S(2)}, u32[]{:S(2)}) collective-permute-start(bf16[512,128]{1,0:T(8,128)(2,1)S(1)} %slice.9), channel_id=1, source_target_pairs={{0,28},{4,0},{8,4},{12,8},{16,12},{20,16},{24,20},{28,24},{1,29},{... | collective-permute-start | bytes 393224 | tf_op jit(solution)/shard_map/ppermute | solution.py:358
  50.5 22.5 %slice-start = ((s8[8388608]{0:T(1024)(128)(4,1)}), s8[4194304]{0:T(1024)(128)(4,1)S(1)}, s32[]{:S(2)}) async-start(s8[8388608]{0:T(1024)(128)(4,1)} %bitcast.5), calls=%async_computation | async-start | bytes 8388608
  54.8 13.5 %collective-permute-start.12 = (bf16[144,768]{1,0:T(8,128)(2,1)S(1)}, bf16[144,768]{1,0:T(8,128)(2,1)S(1)}, u32[]{:S(2)}, u32[]{:S(2)}) collective-permute-start(bf16[144,768]{1,0:T(8,128)(2,1)S(1)} %get-tuple-element.136), channel_id=1, source_target_pairs={{0,96},{32,64},{64,32},{96,0},{128,224},{160,192},{192,160},{224,1... | collective-permute-start | bytes 663560 | tf_op jit(solution)/shard_map/ppermute | solution.py:369
  58.6 10.2 %collective-permute-start.13 = (bf16[144,768]{1,0:T(8,128)(2,1)S(1)}, bf16[144,768]{1,0:T(8,128)(2,1)S(1)}, u32[]{:S(2)}, u32[]{:S(2)}) collective-permute-start(bf16[144,768]{1,0:T(8,128)(2,1)S(1)} %get-tuple-element.137), channel_id=1, source_target_pairs={{0,64},{64,0},{128,192},{192,128},{1,65},{65,1},{129,193},{193,129... | collective-permute-start | bytes 663560 | tf_op jit(solution)/shard_map/ppermute | solution.py:358
  58.6 10.2 %collective-permute-start.14 = (bf16[144,768]{1,0:T(8,128)(2,1)S(1)}, bf16[144,768]{1,0:T(8,128)(2,1)S(1)}, u32[]{:S(2)}, u32[]{:S(2)}) collective-permute-start(bf16[144,768]{1,0:T(8,128)(2,1)S(1)} %get-tuple-element.138), channel_id=1, source_target_pairs={{0,32},{32,0},{1,33},{33,1},{2,34},{34,2},{3,35},{35,3},{4,36},{36... | collective-permute-start | bytes 663560 | tf_op jit(solution)/shard_map/ppermute | solution.py:358
  59.2 13.7 %slice-start.1 = ((s8[8388608]{0:T(1024)(128)(4,1)}), s8[4194304]{0:T(1024)(128)(4,1)S(1)}, s32[]{:S(2)}) async-start(s8[8388608]{0:T(1024)(128)(4,1)} %bitcast.5), calls=%async_computation.1 | async-start | bytes 8388608
  66.1 10.2 %collective-permute-start.15 = (bf16[144,768]{1,0:T(8,128)(2,1)S(1)}, bf16[144,768]{1,0:T(8,128)(2,1)S(1)}, u32[]{:S(2)}, u32[]{:S(2)}) collective-permute-start(bf16[144,768]{1,0:T(8,128)(2,1)S(1)} %get-tuple-element.159), channel_id=1, source_target_pairs={{0,96},{32,64},{64,32},{96,0},{128,224},{160,192},{192,160},{224,1... | collective-permute-start | bytes 663560 | tf_op jit(solution)/shard_map/ppermute | solution.py:369
  68.2 8.0 %collective-permute-start.16 = (bf16[144,768]{1,0:T(8,128)(2,1)S(1)}, bf16[144,768]{1,0:T(8,128)(2,1)S(1)}, u32[]{:S(2)}, u32[]{:S(2)}) collective-permute-start(bf16[144,768]{1,0:T(8,128)(2,1)S(1)} %get-tuple-element.160), channel_id=1, source_target_pairs={{0,64},{64,0},{128,192},{192,128},{1,65},{65,1},{129,193},{193,129... | collective-permute-start | bytes 663560 | tf_op jit(solution)/shard_map/ppermute | solution.py:358
  68.3 8.0 %collective-permute-start.17 = (bf16[144,768]{1,0:T(8,128)(2,1)S(1)}, bf16[144,768]{1,0:T(8,128)(2,1)S(1)}, u32[]{:S(2)}, u32[]{:S(2)}) collective-permute-start(bf16[144,768]{1,0:T(8,128)(2,1)S(1)} %get-tuple-element.161), channel_id=1, source_target_pairs={{0,32},{32,0},{1,33},{33,1},{2,34},{34,2},{3,35},{35,3},{4,36},{36... | collective-permute-start | bytes 663560 | tf_op jit(solution)/shard_map/ppermute | solution.py:358
  76.3 5.7 %collective-permute-start.18 = (bf16[48,4096]{1,0:T(8,128)(2,1)S(1)}, bf16[48,4096]{1,0:T(8,128)(2,1)S(1)}, u32[]{:S(2)}, u32[]{:S(2)}) collective-permute-start(bf16[48,4096]{1,0:T(8,128)(2,1)S(1)} %get-tuple-element.162), channel_id=1, source_target_pairs={{0,1},{1,0},{2,3},{3,2},{4,5},{5,4},{6,7},{7,6},{8,9},{9,8},{10,11... | collective-permute-start | bytes 1179656 | tf_op jit(solution)/shard_map/ppermute | solution.py:358
  82.1 13.8 %collective-permute-start.19 = (bf16[48,4096]{1,0:T(8,128)(2,1)S(1)}, bf16[48,4096]{1,0:T(8,128)(2,1)S(1)}, u32[]{:S(2)}, u32[]{:S(2)}) collective-permute-start(bf16[48,4096]{1,0:T(8,128)(2,1)S(1)} %total.2), channel_id=1, source_target_pairs={{0,2},{2,0},{1,3},{3,1},{4,6},{6,4},{5,7},{7,5},{8,10},{10,8},{9,1... | collective-permute-start | bytes 1179656 | tf_op jit(solution)/shard_map/ppermute | solution.py:358
  94.1 2.1 %collective-permute-start.20 = (bf16[48,4096]{1,0:T(8,128)(2,1)S(1)}, bf16[48,4096]{1,0:T(8,128)(2,1)S(1)}, u32[]{:S(2)}, u32[]{:S(2)}) collective-permute-start(bf16[48,4096]{1,0:T(8,128)(2,1)S(1)} %get-tuple-element.174), channel_id=1, source_target_pairs={{0,1},{1,0},{2,3},{3,2},{4,5},{5,4},{6,7},{7,6},{8,9},{9,8},{10,11... | collective-permute-start | bytes 1179656 | tf_op jit(solution)/shard_map/ppermute | solution.py:358
